TPU v7x, 1024 devices: a whole 4x8x16 slice. The times are simulated.
1024 devices in a mesh: section: 16 (over x, y_hi), ep: 64 (over z, y_lo, core).
Axes of the slice: x: 4, y: 8 (y_hi: 4, y_lo: 2; y = y_hi * 2 + y_lo), z: 16, core: 2. Of those that a mesh axis runs over, the one named last changes fastest.
Arguments:
- tokens_a: bfloat16 [4096, 3584], P(('section', 'ep')), may hold values from -6 to 6
- tokens_b: bfloat16 [4096, 3584], P(('section', 'ep')), may hold values from -6 to 6
- routes_a: int32 [4096, 2], P(('section', 'ep')), may hold values from 0 to 3, all different within a row; in each aligned block of 4 rows (0 to 3, 4 to 7, ...) at most 2 rows name the same one
- routes_b: int32 [4096, 2], P(('section', 'ep')), may hold values from 0 to 3, all different within a row; in each aligned block of 4 rows (0 to 3, 4 to 7, ...) at most 2 rows name the same one
- gains_a: float32 [4096, 2], P(('section', 'ep')), may hold values from 0.3 to 1.5
- gains_b: float32 [4096, 2], P(('section', 'ep')), may hold values from 0.3 to 1.5
- w_gate_up: bfloat16 [16, 3584, 2, 8192], P('section', None, None, 'ep'), may hold values from -0.09375 to 0.09375
- w_down: bfloat16 [16, 8192, 3584], P('section', 'ep'), may hold values from -0.125 to 0.125
Outputs:
- mixed_a: bfloat16 [4096, 3584], P(('section', 'ep'))
- mixed_b: bfloat16 [4096, 3584], P(('section', 'ep'))
Inputs may be any that keep to these rules, and one draw needn't show every extreme that they name: `routes_a`: each row names 2 different experts. Among the 4 rows of one device, no expert is named more than 2 times, and in every draw some device's rows name some expert exactly 2 times. `routes_b`: as for routes_a.
All inputs are finite; a program needn't handle non-finite values.
Results may differ from a plain program's by a relative error of at most 0.0065.
Values may be sent and summed in bfloat16 or wider, within the bound.
A program may use at most 32 MiB of HBM per device.

v0:
```python
import jax
import jax.numpy as jnp
from jax import lax
from jax.sharding import PartitionSpec as P

EXPERTS = 4
TOP = 2
TOK_DEV = 4
CAP = 2


def from_behind(shard, axis, by):
    length = lax.axis_size(axis)
    pairs = [(i, i + by) for i in range(length) if 0 <= i + by < length]
    return lax.ppermute(shard, axis, pairs)


def route_slots(routes_flat):
    onehot = (routes_flat[:, None] == jnp.arange(EXPERTS, dtype=jnp.int32)[None, :]).astype(
        jnp.int32
    )
    return jnp.sum((jnp.cumsum(onehot, axis=0) - 1) * onehot, axis=1)


def shards(tokens_a, tokens_b, routes_a, routes_b, gains_a, gains_b, w_gate_up, w_down):
    group = lax.axis_size("ep") // EXPERTS
    width = w_down.shape[1]
    model_width = tokens_a.shape[1]
    united = w_gate_up[0].reshape(model_width, 2 * width)
    down = w_down[0]
    last_section = lax.axis_size("section") - 1
    results = []
    for tokens, routes, gains, step_by, edge in (
        (tokens_a, routes_a, gains_a, 1, 0),
        (tokens_b, routes_b, gains_b, -1, last_section),
    ):
        received = from_behind(tokens, "section", step_by)
        prepare_current = jnp.where(lax.axis_index("section") == edge, tokens, received)
        route_ids = routes.reshape(-1)
        slot_ids = route_slots(route_ids)
        expert_ids = jnp.arange(EXPERTS, dtype=jnp.int32)
        slot_range = jnp.arange(CAP, dtype=jnp.int32)
        prepare_chosen = (route_ids[None, None, :] == expert_ids[:, None, None]) & (
            slot_ids[None, None, :] == slot_range[None, :, None]
        )
        prepare_chosen = prepare_chosen.reshape(EXPERTS, CAP, TOK_DEV, TOP)
        picker = jnp.sum(prepare_chosen.astype(jnp.int32), axis=3).astype(jnp.bfloat16)
        packed = jnp.einsum(
            "ect,td->ecd", picker, prepare_current, preferred_element_type=jnp.float32
        ).astype(jnp.bfloat16)
        outgoing = jnp.repeat(packed, group, axis=0)
        arrived = lax.all_to_all(outgoing, "ep", split_axis=0, concat_axis=0, tiled=True)
        inputs = arrived.reshape(-1, model_width)
        projected = jnp.dot(inputs, united, preferred_element_type=jnp.float32)
        hidden = (jax.nn.silu(projected[:, :width]) * projected[:, width:]).astype(jnp.bfloat16)
        partial_value = jnp.dot(hidden, down, preferred_element_type=jnp.float32).astype(
            jnp.bfloat16
        )
        returned = lax.all_to_all(
            partial_value.reshape(arrived.shape), "ep", split_axis=0, concat_axis=0, tiled=True
        )
        summed = jnp.sum(
            returned.reshape(EXPERTS, group, CAP, model_width).astype(jnp.float32), axis=1
        )
        weighting = jnp.sum(prepare_chosen.astype(jnp.float32) * gains[None, None, :, :], axis=3)
        mixed = prepare_current.astype(jnp.float32) + jnp.einsum(
            "ect,ecd->td", weighting, summed, precision=lax.Precision.HIGHEST
        )
        results.append(mixed.astype(jnp.bfloat16))
    mixed_a, mixed_b = (results[0], results[1])
    return (mixed_a, mixed_b)


def solution(mesh):
    in_specs = (
        P(("section", "ep"), None),
        P(("section", "ep"), None),
        P(("section", "ep"), None),
        P(("section", "ep"), None),
        P(("section", "ep"), None),
        P(("section", "ep"), None),
        P("section", None, None, "ep"),
        P("section", "ep", None),
    )
    out_specs = (P(("section", "ep"), None), P(("section", "ep"), None))
    return jax.shard_map(shards, mesh=mesh, in_specs=in_specs, out_specs=out_specs, check_vma=False)
```

profile of v0, /device:TPU:1, one launch (start us, length us, event | category | flops | bytes accessed | tf_op | source)
XLA Modules:
  0.0 249.3 jit_solution(7527996975527187770)
XLA Ops:
  0.7 1.4 collective-permute-start.1
  2.1 0.8 copy.41
  4.1 3.3 %collective-permute-done.1 = bf16[4,3584]{1,0:T(4,128)(2,1)S(1)} collective-permute-done((bf16[4,3584]{1,0:T(4,128)(2,1)}, bf16[4,3584]{1,0:T(4,128)(2,1)S(1)}, u32[]{:S(2)}, u32[]{:S(2)}) %collective-permute-start.1) | collective-permute-done | bytes 28704 | tf_op jit(solution)/shard_map/ppermute | solution.py:15
  7.5 1.4 broadcast_in_dim.5
  8.9 22.2 %all-to-all-start.2 = ((bf16[64,2,3584]{2,1,0:T(2,128)(2,1)}), bf16[64,2,3584]{2,1,0:T(2,128)(2,1)S(1)}, u32[]{:S(2)}, u32[]{:S(2)}) async-start(bf16[64,2,3584]{2,1,0:T(2,128)(2,1)} %bitcast.6), calls=%async_computation.2 | async-start | bytes 1835008 | tf_op jit(solution)/shard_map/all_to_all | solution.py:52
  31.1 5.6 %collective-permute-start = (bf16[4,3584]{1,0:T(4,128)(2,1)S(1)}, bf16[4,3584]{1,0:T(4,128)(2,1)S(1)}, u32[]{:S(2)}, u32[]{:S(2)}) collective-permute-start(bf16[4,3584]{1,0:T(4,128)(2,1)S(1)} %copy-done.2), channel_id=1, source_target_pairs={{0,64},{64,128},{128,192},{192,256},{256,320},{320,384},{384,448},... | collective-permute-start | bytes 86024 | tf_op jit(solution)/shard_map/ppermute | solution.py:15
  37.9 41.7 %all-to-all-done.2 = bf16[64,2,3584]{2,1,0:T(2,128)(2,1)S(1)} async-done(((bf16[64,2,3584]{2,1,0:T(2,128)(2,1)}), bf16[64,2,3584]{2,1,0:T(2,128)(2,1)S(1)}, u32[]{:S(2)}, u32[]{:S(2)}) %all-to-all-start.2) | async-done | bytes 917536 | tf_op jit(solution)/shard_map/all_to_all | solution.py:52
  79.6 1.4 broadcast_in_dim.4
  81.0 6.6 %all-to-all-start = ((bf16[64,2,3584]{2,1,0:T(2,128)(2,1)}), bf16[64,2,3584]{2,1,0:T(2,128)(2,1)S(1)}, u32[]{:S(2)}, u32[]{:S(2)}) async-start(bf16[64,2,3584]{2,1,0:T(2,128)(2,1)} %bitcast.34), calls=%async_computation | async-start | bytes 1835008 | tf_op jit(solution)/shard_map/all_to_all | solution.py:52
  87.6 1.3 reshape.148
  88.9 2.2 fusion
  91.5 1.3 reshape.149
  92.8 43.5 %all-to-all-done = bf16[64,2,3584]{2,1,0:T(2,128)(2,1)S(1)} async-done(((bf16[64,2,3584]{2,1,0:T(2,128)(2,1)}), bf16[64,2,3584]{2,1,0:T(2,128)(2,1)S(1)}, u32[]{:S(2)}, u32[]{:S(2)}) %all-to-all-start) | async-done | bytes 917536 | tf_op jit(solution)/shard_map/all_to_all | solution.py:52
  136.2 6.6 %all-to-all-start.3 = ((bf16[64,2,3584]{2,1,0:T(2,128)(2,1)}), bf16[64,2,3584]{2,1,0:T(2,128)(2,1)S(1)}, u32[]{:S(2)}, u32[]{:S(2)}) async-start(bf16[64,2,3584]{2,1,0:T(2,128)(2,1)} %reshape.149), calls=%async_computation.3 | async-start | bytes 1835008 | tf_op jit(solution)/shard_map/all_to_all | solution.py:59
  142.8 1.3 reshape.145
  144.1 2.2 fusion.2
  146.8 1.3 reshape.146
  148.1 43.4 %all-to-all-done.3 = bf16[64,2,3584]{2,1,0:T(2,128)(2,1)S(1)} async-done(((bf16[64,2,3584]{2,1,0:T(2,128)(2,1)}), bf16[64,2,3584]{2,1,0:T(2,128)(2,1)S(1)}, u32[]{:S(2)}, u32[]{:S(2)}) %all-to-all-start.3) | async-done | bytes 917536 | tf_op jit(solution)/shard_map/all_to_all | solution.py:59
  191.5 6.6 %all-to-all-start.1 = ((bf16[64,2,3584]{2,1,0:T(2,128)(2,1)}), bf16[64,2,3584]{2,1,0:T(2,128)(2,1)S(1)}, u32[]{:S(2)}, u32[]{:S(2)}) async-start(bf16[64,2,3584]{2,1,0:T(2,128)(2,1)} %reshape.146), calls=%async_computation.1 | async-start | bytes 1835008 | tf_op jit(solution)/shard_map/all_to_all | solution.py:59
  198.1 0.8 convert_reduce_fusion
  198.9 47.8 %all-to-all-done.1 = bf16[64,2,3584]{2,1,0:T(2,128)(2,1)S(1)} async-done(((bf16[64,2,3584]{2,1,0:T(2,128)(2,1)}), bf16[64,2,3584]{2,1,0:T(2,128)(2,1)S(1)}, u32[]{:S(2)}, u32[]{:S(2)}) %all-to-all-start.1) | async-done | bytes 917536 | tf_op jit(solution)/shard_map/all_to_all | solution.py:59
  246.7 0.8 convert_reduce_fusion.1
  247.4 0.9 add_convert_fusion
  248.4 0.9 add_convert_fusion.1
  (40 shorter events, 3.3 us)
Async XLA Ops:
  0.6 90.5 %copy-start = (bf16[1,128,3584]{2,1,0:T(8,128)(2,1)S(1)}, bf16[1,128,3584]{2,1,0:T(8,128)(2,1)}, u32[]{:S(2)}) copy-start(bf16[1,128,3584]{2,1,0:T(8,128)(2,1)} %param.15) | copy-start | bytes 2752516
  0.6 30.5 %copy-start.2 = (bf16[4,3584]{1,0:T(4,128)(2,1)S(1)}, bf16[4,3584]{1,0:T(4,128)(2,1)}, u32[]{:S(2)}) copy-start(bf16[4,3584]{1,0:T(4,128)(2,1)} %param.8) | copy-start | bytes 86020
  0.7 36.1 %copy-start.3 = (s32[4,2]{0,1:T(2,128)S(1)}, s32[4,2]{0,1:T(2,128)}, u32[]{:S(2)}) copy-start(s32[4,2]{0,1:T(2,128)} %param.10) | copy-start | bytes 100
  0.7 6.6 %collective-permute-start.1 = (bf16[4,3584]{1,0:T(4,128)(2,1)}, bf16[4,3584]{1,0:T(4,128)(2,1)S(1)}, u32[]{:S(2)}, u32[]{:S(2)}) collective-permute-start(bf16[4,3584]{1,0:T(4,128)(2,1)} %param.9), channel_id=1, source_target_pairs={{64,0},{128,64},{192,128},{256,192},{320,256},{384,320},{448,384},... | collective-permute-start | bytes 86024 | tf_op jit(solution)/shard_map/ppermute | solution.py:15
  8.9 70.7 %all-to-all-start.2 = ((bf16[64,2,3584]{2,1,0:T(2,128)(2,1)}), bf16[64,2,3584]{2,1,0:T(2,128)(2,1)S(1)}, u32[]{:S(2)}, u32[]{:S(2)}) async-start(bf16[64,2,3584]{2,1,0:T(2,128)(2,1)} %bitcast.6), calls=%async_computation.2 | async-start | bytes 1835008 | tf_op jit(solution)/shard_map/all_to_all | solution.py:52
  31.1 6.6 %collective-permute-start = (bf16[4,3584]{1,0:T(4,128)(2,1)S(1)}, bf16[4,3584]{1,0:T(4,128)(2,1)S(1)}, u32[]{:S(2)}, u32[]{:S(2)}) collective-permute-start(bf16[4,3584]{1,0:T(4,128)(2,1)S(1)} %copy-done.2), channel_id=1, source_target_pairs={{0,64},{64,128},{128,192},{192,256},{256,320},{320,384},{384,448},... | collective-permute-start | bytes 86024 | tf_op jit(solution)/shard_map/ppermute | solution.py:15
  81.0 55.2 %all-to-all-start = ((bf16[64,2,3584]{2,1,0:T(2,128)(2,1)}), bf16[64,2,3584]{2,1,0:T(2,128)(2,1)S(1)}, u32[]{:S(2)}, u32[]{:S(2)}) async-start(bf16[64,2,3584]{2,1,0:T(2,128)(2,1)} %bitcast.34), calls=%async_computation | async-start | bytes 1835008 | tf_op jit(solution)/shard_map/all_to_all | solution.py:52
  136.2 55.2 %all-to-all-start.3 = ((bf16[64,2,3584]{2,1,0:T(2,128)(2,1)}), bf16[64,2,3584]{2,1,0:T(2,128)(2,1)S(1)}, u32[]{:S(2)}, u32[]{:S(2)}) async-start(bf16[64,2,3584]{2,1,0:T(2,128)(2,1)} %reshape.149), calls=%async_computation.3 | async-start | bytes 1835008 | tf_op jit(solution)/shard_map/all_to_all | solution.py:59
  146.7 51.3 %copy-start.4 = (f32[4,2]{0,1:T(2,128)S(1)}, f32[4,2]{0,1:T(2,128)}, u32[]{:S(2)}) copy-start(f32[4,2]{0,1:T(2,128)} %param.13) | copy-start | bytes 100
  146.8 51.3 %copy-start.5 = (f32[4,2]{0,1:T(2,128)S(1)}, f32[4,2]{0,1:T(2,128)}, u32[]{:S(2)}) copy-start(f32[4,2]{0,1:T(2,128)} %param.12) | copy-start | bytes 100
  148.1 99.4 %copy-start.1 = (bf16[4,3584]{1,0:T(4,128)(2,1)S(1)}, bf16[4,3584]{1,0:T(4,128)(2,1)}, u32[]{:S(2)}) copy-start(bf16[4,3584]{1,0:T(4,128)(2,1)} %param.9) | copy-start | bytes 86020
  191.5 55.2 %all-to-all-start.1 = ((bf16[64,2,3584]{2,1,0:T(2,128)(2,1)}), bf16[64,2,3584]{2,1,0:T(2,128)(2,1)S(1)}, u32[]{:S(2)}, u32[]{:S(2)}) async-start(bf16[64,2,3584]{2,1,0:T(2,128)(2,1)} %reshape.146), calls=%async_computation.1 | async-start | bytes 1835008 | tf_op jit(solution)/shard_map/all_to_all | solution.py:59
where the time goes:
time: 253 us; the launch traced here: 249 us
  waiting for transfers between devices  180 us (71%)
  starting transfers between devices  49 us (19%)
  local copies, waits for them, and re-layouts  9.53 us (4%)
  matrix products  7.34 us (3%)
  other arithmetic  2.74 us (1%)
    all_to_all x2, waiting for transfers between devices, shards(): lax.all_to_all(partial_value.reshape(arrived.shape), 'ep', split_axis=0,...  91.2 us
    all_to_all x2, waiting for transfers between devices, shards(): lax.all_to_all(outgoing, 'ep', split_axis=0, concat_axis=0, tiled=True)  85.1 us
    all_to_all x2, starting transfers between devices, shards(): lax.all_to_all(outgoing, 'ep', split_axis=0, concat_axis=0, tiled=True)  28.8 us
    all_to_all x2, starting transfers between devices, shards(): lax.all_to_all(partial_value.reshape(arrived.shape), 'ep', split_axis=0,...  13.2 us
    ppermute x2, starting transfers between devices, from_behind(): return lax.ppermute(shard, axis, pairs)  7.04 us
  transfers between devices with their start and end apart: 6, of which 6 were waited for; matrix products, arithmetic and copies ran while one was open for 6% of the time, Pallas kernels for 0%

commit v1 on v0

v1 whole, which is shorter than its diff:
```python
import functools

import jax
import jax.numpy as jnp
from jax import lax
from jax.experimental import pallas as pl
from jax.experimental.pallas import tpu as pltpu
from jax.sharding import PartitionSpec as P

EXPERTS = 4
TOP = 2
TOK = 4
CAP = 2
QUARTERS = 4
PER_GROUP = 4
LEAD = 2
BF16 = jnp.bfloat16
F32 = jnp.float32


def slot_order(nz):
    order = [0]
    for step in range(1, nz // 2):
        order += [step, nz - step]
    return order + [nz // 2]


class Copies:
    def __init__(self, send_sems, recv_sems):
        self.send_sems, self.recv_sems, self.used = send_sems, recv_sems, 0

    def make(self, src, dst, device):
        index = self.used
        self.used += 1
        return pltpu.make_async_remote_copy(
            src_ref=src,
            dst_ref=dst,
            send_sem=self.send_sems.at[index],
            recv_sem=self.recv_sems.at[index],
            device_id=device,
            device_id_type=pl.DeviceIdType.MESH,
        )


def n_copies(nz):
    half, groups = nz // 2, nz // PER_GROUP
    ring = 2 * (2 * half - 1)
    return 2 + (2 * half - 1) + 2 * ring + 3 * groups + 2 * groups


def iota(shape, dim):
    return lax.broadcasted_iota(jnp.int32, shape, dim)


def kernel(
    ns,
    nz,
    d,
    tok_a,
    tok_b,
    routes_a,
    routes_b,
    gains_a,
    gains_b,
    wgu_hbm,
    wd_hbm,
    out_a,
    out_b,
    outgoing,
    ring,
    meta,
    x,
    wgu_raw,
    wgu,
    wd,
    p_own,
    p_send,
    p_recv,
    y_send,
    y_recv,
    expand,
    gain_col,
    contrib,
    rs_send,
    rs_recv,
    send_sems,
    recv_sems,
    local_sems,
):
    q = d // QUARTERS
    half = nz // 2
    groups = nz // PER_GROUP
    order = slot_order(nz)
    pos = {r: i for i, r in enumerate(order)}

    section = lax.axis_index("section")
    ep = lax.axis_index("ep")
    z, low = ep // 4, ep % 4
    y, core = low // 2, low % 2
    expert = z // (nz // EXPERTS)
    right = (section, lax.rem(z + 1, nz) * 4 + low)
    left = (section, lax.rem(z + nz - 1, nz) * 4 + low)
    across = (section, ep + 2 - 4 * y)
    twin = (section, ep + 1 - 2 * core)
    up = (section + 1, ep)
    down = (section - 1, ep)
    not_last = section < ns - 1
    not_first = section > 0

    load_gu = pltpu.make_async_copy(wgu_hbm.at[0], wgu_raw, local_sems.at[0])
    load_d = pltpu.make_async_copy(wd_hbm.at[0], wd, local_sems.at[1])
    load_gu.start()
    load_d.start()

    barrier = pltpu.get_barrier_semaphore()
    for peer in (right, left, across, twin):
        pl.semaphore_signal(barrier, inc=1, device_id=peer, device_id_type=pl.DeviceIdType.MESH)

    @pl.when(not_last)
    def _():
        pl.semaphore_signal(barrier, inc=1, device_id=up, device_id_type=pl.DeviceIdType.MESH)

    @pl.when(not_first)
    def _():
        pl.semaphore_signal(barrier, inc=1, device_id=down, device_id_type=pl.DeviceIdType.MESH)

    for stream, tok in enumerate((tok_a, tok_b)):
        rows = tok[...].astype(F32)
        outgoing[stream] = jnp.concatenate(
            [rows[:, i * q : (i + 1) * q] for i in range(QUARTERS)], axis=0
        ).astype(BF16)

    lane = iota((1, 128), 1)
    lane_stream = (lane // 8) % 2
    lane_expert = (lane // CAP) % EXPERTS
    lane_slot = lane % CAP
    count = jnp.zeros((1, 128), jnp.int32)
    token = jnp.zeros((1, 128), F32)
    gain = jnp.zeros((1, 128), F32)
    for t in range(TOK):
        for k in range(TOP):
            route = jnp.where(lane_stream == 0, routes_a[t, k], routes_b[t, k])
            value = jnp.where(lane_stream == 0, gains_a[t, k], gains_b[t, k])
            named = route == lane_expert
            here = named & (count == lane_slot)
            token = jnp.where(here, float(t), token)
            gain = jnp.where(here, value, gain)
            count = count + named.astype(jnp.int32)
    meta[0] = jnp.where(lane < 16, token, gain)

    copies = Copies(send_sems, recv_sems)
    relay_up = copies.make(outgoing.at[0], ring.at[0, 0], up)
    relay_down = copies.make(outgoing.at[1], ring.at[0, 1], down)
    plus, minus = [{}, {}], [{}, {}]
    for j in range(1, half + 1):
        for s in range(2):
            if j < half or s == 0:
                plus[s][j] = copies.make(ring.at[pos[j - 1], s], ring.at[pos[j], s], right)
            if j < half or s == 1:
                minus[s][j] = copies.make(
                    ring.at[pos[(nz - j + 1) % nz], s], ring.at[pos[nz - j], s], left
                )
    meta_plus, meta_minus = {}, {}
    for j in range(1, half + 1):
        meta_plus[j] = copies.make(meta.at[pos[j - 1]], meta.at[pos[j]], right)
        if j < half:
            meta_minus[j] = copies.make(meta.at[pos[(nz - j + 1) % nz]], meta.at[pos[nz - j]], left)

    x_across = [copies.make(x.at[k, 0], x.at[k, 2], across) for k in range(groups)]
    x_twin = [copies.make(x.at[k, 0], x.at[k, 1], twin) for k in range(groups)]
    x_far = [copies.make(x.at[k, 2], x.at[k, 3], twin) for k in range(groups)]
    p_twin = [copies.make(p_send.at[k], p_recv.at[k], twin) for k in range(groups)]
    p_across = [copies.make(y_send.at[k], y_recv.at[k], across) for k in range(groups)]
    back = [[{}, {}], [{}, {}]]
    for j in range(1, half + 1):
        for way, device in enumerate((right, left)):
            for s in range(2):
                if j > 1 or s == way:
                    back[way][s][j] = copies.make(
                        rs_send.at[way, j - 1, s], rs_recv.at[way, j - 1, s], device
                    )

    pl.semaphore_wait(barrier, 4 + not_last.astype(jnp.int32) + not_first.astype(jnp.int32))

    @pl.when(not_last)
    def _():
        relay_up.start()

    @pl.when(not_first)
    def _():
        relay_down.start()

    meta_plus[1].start()
    meta_minus[1].start()

    @pl.when(section == 0)
    def _():
        ring[0, 0] = outgoing[0]

    @pl.when(section == ns - 1)
    def _():
        ring[0, 1] = outgoing[1]

    def meta_step(j):
        for ways in (meta_plus, meta_minus):
            if j in ways:
                ways[j].wait_recv()
                if j + 1 in ways:
                    ways[j + 1].start()

    for j in range(1, LEAD + 1):
        meta_step(j)

    @pl.when(not_first)
    def _():
        relay_up.wait_recv()

    plus[0][1].start()
    minus[0][1].start()

    @pl.when(not_last)
    def _():
        relay_down.wait_recv()

    plus[1][1].start()
    minus[1][1].start()

    def spread_meta(k, rows, row_src):
        spread = jnp.zeros((rows, 128), F32)
        for s in range(PER_GROUP):
            spread = jnp.where(row_src == s, meta[k * PER_GROUP + s], spread)
        return spread

    def select(k):
        row, col = iota((64, 128), 0), iota((64, 128), 1)
        row_q, row_src, row_st, row_sl = row // 16, (row // 4) % 4, (row // 2) % 2, row % 2
        spread = spread_meta(k, 64, row_src)
        want = row_st * 8 + expert * CAP + row_sl
        tok = jnp.sum(jnp.where(col == want, spread, 0.0), axis=1, keepdims=True)
        target = (row_src * 32 + row_st * 16 + row_q * 4).astype(F32) + tok
        picker = jnp.where(col.astype(F32) == target, 1.0, 0.0).astype(BF16)
        rows = ring[k * PER_GROUP : (k + 1) * PER_GROUP].reshape(PER_GROUP * 2 * 16, q)
        picked = jnp.dot(picker, rows, preferred_element_type=F32)
        for i in range(QUARTERS):
            x[k, 0, :, i * q : (i + 1) * q] = picked[i * 16 : (i + 1) * 16].astype(BF16)

    def prepare_expand(k):
        row, col = iota((128, 128), 0), iota((128, 128), 1)
        row_src, row_st, row_q, row_t = row // 32, (row // 16) % 2, (row // 4) % 4, row % 4
        col_q, col_src = (col // 16) % 4, (col // 4) % 4
        col_st, col_sl = (col // 2) % 2, col % 2
        spread = spread_meta(k, 128, row_src)
        want = row_st * 8 + expert * CAP
        tok0 = jnp.sum(jnp.where(col == want, spread, 0.0), axis=1, keepdims=True)
        tok1 = jnp.sum(jnp.where(col == want + 1, spread, 0.0), axis=1, keepdims=True)
        tok = jnp.where(col_sl == 0, tok0, tok1)
        same = (row_q == col_q) & (row_src == col_src) & (row_st == col_st)
        expand[k] = jnp.where(same & (tok == row_t.astype(F32)), 1.0, 0.0).astype(BF16)
        row, col = iota((16, 128), 0), iota((16, 128), 1)
        spread = spread_meta(k, 16, row // 4)
        want = 16 + ((row // 2) % 2) * 8 + expert * CAP + row % 2
        gains = jnp.sum(jnp.where(col == want, spread, 0.0), axis=1, keepdims=True)
        gain_col[k] = jnp.broadcast_to(gains, (16, 128))

    def experts(k):
        hidden_in = jnp.dot(x[k].reshape(64, d), wgu[...], preferred_element_type=F32)
        gate, upper = hidden_in[:, :128], hidden_in[:, 128:]
        hidden = (gate * jax.nn.sigmoid(gate) * upper).astype(BF16)
        part = jnp.dot(hidden, wd[...], preferred_element_type=F32)
        p_own[k, 0] = part[0:16]
        p_send[k, 0] = part[16:32].astype(BF16)
        p_own[k, 1] = part[32:48]
        p_send[k, 1] = part[48:64].astype(BF16)
        p_twin[k].start()

    def unpack_weights(i, carry):
        rows = pl.ds(pl.multiple_of(i * 256, 256), 256)
        wgu[rows, :] = wgu_raw[rows].reshape(256, wgu.shape[1])
        return carry

    for j in range(1, half + 1):
        for s in range(2):
            for ways in (plus, minus):
                if j in ways[s]:
                    ways[s][j].wait_recv()
                    if j + 1 in ways[s]:
                        ways[s][j + 1].start()
        meta_step(j + LEAD)
        if j == 1:
            load_gu.wait()
            lax.fori_loop(0, d // 256, unpack_weights, 0)
            load_d.wait()
        if j % 2 == 0:
            k = j // 2 - 1
            select(k)
            x_across[k].start()
            x_twin[k].start()
            prepare_expand(k)
            if k > 0:
                x_across[k - 1].wait_recv()
                x_far[k - 1].start()
        elif j > 3:
            k = (j - 5) // 2
            x_twin[k].wait_recv()
            x_far[k].wait_recv()
            experts(k)

    last = groups - 1
    if groups > 1:
        x_twin[last - 1].wait_recv()
        x_far[last - 1].wait_recv()
        experts(last - 1)
    x_across[last].wait_recv()
    x_far[last].start()
    x_twin[last].wait_recv()
    x_far[last].wait_recv()
    experts(last)

    def sum_twins(k):
        p_twin[k].wait_recv()
        y_send[k] = (p_own[k, 1] + p_recv[k, 1].astype(F32)).astype(BF16)
        p_across[k].start()
        p_own[k, 0] = p_own[k, 0] + p_recv[k, 0].astype(F32)

    def to_tokens(k):
        p_across[k].wait_recv()
        total = (p_own[k, 0] + y_recv[k].astype(F32)) * gain_col[k][:, 0:1]
        stacked = jnp.concatenate([total[:, i * q : (i + 1) * q] for i in range(QUARTERS)], axis=0)
        high = stacked.astype(BF16)
        rest = (stacked - high.astype(F32)).astype(BF16)
        spread = jnp.dot(
            expand[k], jnp.concatenate([high, rest], axis=0), preferred_element_type=F32
        )
        contrib[k * PER_GROUP : (k + 1) * PER_GROUP] = spread.reshape(PER_GROUP, 2, 16, q)

    sum_twins(last)
    if groups > 1:
        sum_twins(last - 1)
    for j in range(1, half + 1):
        if j % 2 == 1:
            k = last - j // 2
            to_tokens(k)
            if k > 1:
                sum_twins(k - 2)
        distance = half + 1 - j
        for s in range(2):
            for way in range(2):
                if j in back[way][s]:
                    slot = nz - distance if way == 0 else distance
                    value = contrib[pos[slot % nz], s]
                    if j - 1 in back[way][s]:
                        back[way][s][j - 1].wait_recv()
                        value = value + rs_recv[way, j - 2, s].astype(F32)
                    rs_send[way, j - 1, s] = value.astype(BF16)
                    back[way][s][j].start()

    for s, out in enumerate((out_a, out_b)):
        value = ring[0, s].astype(F32) + contrib[0, s]
        for way in range(2):
            back[way][s][half].wait_recv()
            value = value + rs_recv[way, half - 1, s].astype(F32)
        for i in range(QUARTERS):
            out[:, i * q : (i + 1) * q] = value[i * TOK : (i + 1) * TOK].astype(BF16)

    @pl.when(not_last)
    def _():
        relay_up.wait_send()

    @pl.when(not_first)
    def _():
        relay_down.wait_send()

    every = list(meta_plus.values()) + list(meta_minus.values())
    for ways in (plus, minus, back[0], back[1]):
        every += list(ways[0].values()) + list(ways[1].values())
    for copy in every + x_across + x_twin + x_far + p_twin + p_across:
        copy.wait_send()


def shards(ns, nz, *args):
    tokens_a = args[0]
    d = tokens_a.shape[1]
    q = d // QUARTERS
    half, groups = nz // 2, nz // PER_GROUP
    width = args[7].shape[1]
    n = n_copies(nz)
    vmem = pl.BlockSpec(memory_space=pltpu.VMEM)
    smem = pl.BlockSpec(memory_space=pltpu.SMEM)
    hbm = pl.BlockSpec(memory_space=pl.ANY)
    return pl.pallas_call(
        functools.partial(kernel, ns, nz, d),
        out_shape=[jax.ShapeDtypeStruct(tokens_a.shape, BF16)] * 2,
        in_specs=[vmem] * 2 + [smem] * 4 + [hbm] * 2,
        out_specs=[vmem] * 2,
        scratch_shapes=[
            pltpu.VMEM((2, 16, q), BF16),
            pltpu.VMEM((nz, 2, 16, q), BF16),
            pltpu.VMEM((nz, 1, 128), F32),
            pltpu.VMEM((groups, 4, 16, d), BF16),
            pltpu.VMEM((d, 2, width), BF16),
            pltpu.VMEM((d, 2 * width), BF16),
            pltpu.VMEM((width, d), BF16),
            pltpu.VMEM((groups, 2, 16, d), F32),
            pltpu.VMEM((groups, 2, 16, d), BF16),
            pltpu.VMEM((groups, 2, 16, d), BF16),
            pltpu.VMEM((groups, 16, d), BF16),
            pltpu.VMEM((groups, 16, d), BF16),
            pltpu.VMEM((groups, 128, 128), BF16),
            pltpu.VMEM((groups, 16, 128), F32),
            pltpu.VMEM((nz, 2, 16, q), F32),
            pltpu.VMEM((2, half, 2, 16, q), BF16),
            pltpu.VMEM((2, half, 2, 16, q), BF16),
            pltpu.SemaphoreType.DMA((n,)),
            pltpu.SemaphoreType.DMA((n,)),
            pltpu.SemaphoreType.DMA((2,)),
        ],
        compiler_params=pltpu.CompilerParams(
            collective_id=0, has_side_effects=True, vmem_limit_bytes=60 * 1024 * 1024
        ),
    )(*args)


def solution(mesh):
    ns, nz = mesh.shape["section"], mesh.shape["ep"] // 4
    rows = P(("section", "ep"), None)
    in_specs = (rows,) * 6 + (P("section", None, None, "ep"), P("section", "ep", None))
    return jax.shard_map(
        functools.partial(shards, ns, nz),
        mesh=mesh,
        in_specs=in_specs,
        out_specs=(rows, rows),
        check_vma=False,
    )
```

time: 253 us -> 103 us (0.41)
  the two profiles are of different devices: /device:TPU:1 before, /device:TPU:6 now
where the time goes in v1:
time: 103 us; the launch traced here: 102 us
  Pallas kernels  93.8 us (91%)
  local copies, waits for them, and re-layouts  8.09 us (8%)
    pallas_call x1, Pallas kernels, shards(): pl.pallas_call(functools.partial(kernel, ns, nz, d), out_shape=[jax.Shape...  93.8 us
    unnamed x6, local copies, waits for them, and re-layouts  8.09 us

profile of v1, /device:TPU:6, one launch (start us, length us, event | category | flops | bytes accessed | tf_op | source)
XLA Modules:
  0.0 102.5 jit_solution(984330356962405499)
XLA Ops:
  0.6 1.3 %copy.10.routes_a = s32[4,2]{1,0:T(4,128)} copy(s32[4,2]{0,1:T(2,128)} %param.10) | data formatting | bytes 64 | tf_op args[2]
  2.0 1.3 %copy.11.routes_b = s32[4,2]{1,0:T(4,128)} copy(s32[4,2]{0,1:T(2,128)} %param.11) | data formatting | bytes 64 | tf_op args[3]
  3.3 1.3 %copy.12.gains_a = f32[4,2]{1,0:T(4,128)} copy(f32[4,2]{0,1:T(2,128)} %param.12) | data formatting | bytes 64 | tf_op args[4]
  4.6 1.4 %copy.13.gains_b = f32[4,2]{1,0:T(4,128)} copy(f32[4,2]{0,1:T(2,128)} %param.13) | data formatting | bytes 64 | tf_op args[5]
  6.0 93.8 %shard_map.95 = (bf16[4,3584]{1,0:T(4,128)(2,1)}, bf16[4,3584]{1,0:T(4,128)(2,1)}) custom-call(bf16[4,3584]{1,0:T(4,128)(2,1)} %tok_a.1, bf16[4,3584]{1,0:T(4,128)(2,1)} %tok_b.1, s32[4,2]{1,0:T(4,128)} %copy.10.routes_a, s32[4,2]{1,0:T(4,128)} %copy.11.routes_b, f32[4,2]{1,0:T(4,128)} %copy.12.gains_a, f32[4,2]{1,0:T(4,128)} %copy.13.gains_b, ...), custom_call_target="tpu_custom_call" | custom-call | tf_op jit(solution)/shard_map/pallas_call | solution.py:390
  99.8 1.4 %copy.16 = bf16[4,3584]{1,0:T(4,128)(2,1)} copy(bf16[4,3584]{1,0:T(4,128)(2,1)} %get-tuple-element.4) | data formatting | bytes 57344
  101.1 1.4 %copy.17 = bf16[4,3584]{1,0:T(4,128)(2,1)} copy(bf16[4,3584]{1,0:T(4,128)(2,1)} %get-tuple-element.5) | data formatting | bytes 57344

commit v2 on v0

v2 whole, which is shorter than its diff:
```python
import functools

import jax
import jax.numpy as jnp
from jax import lax
from jax.experimental import pallas as pl
from jax.experimental.pallas import tpu as pltpu
from jax.sharding import PartitionSpec as P

EXPERTS = 4
TOP = 2
TOK = 4
CAP = 2
QUARTERS = 4
LINE = 4
NZ = EXPERTS * LINE
BF16 = jnp.bfloat16
F32 = jnp.float32
MESH = pl.DeviceIdType.MESH
N_SEMS = 80


def iota(shape, dim):
    return lax.broadcasted_iota(jnp.int32, shape, dim)


def find_tokens(routes, gains, stream, expert, slot):
    count = jnp.zeros(stream.shape, jnp.int32)
    token = jnp.zeros(stream.shape, jnp.int32)
    gain = jnp.zeros(stream.shape, F32)
    for t in range(TOK):
        for k in range(TOP):
            route = jnp.where(stream == 0, routes[0][k, t], routes[1][k, t])
            named = route == expert
            here = named & (count == slot)
            token = jnp.where(here, t, token)
            if gains is not None:
                value = jnp.where(stream == 0, gains[0][k, t], gains[1][k, t])
                gain = jnp.where(here, value, gain)
            count = count + named.astype(jnp.int32)
    return token, gain


def kernel(
    ns,
    d,
    tok_a,
    tok_b,
    routes_a,
    routes_b,
    gains_a,
    gains_b,
    wgu_hbm,
    wd_hbm,
    out_a,
    out_b,
    outgoing,
    current,
    packed,
    xin,
    wgu_raw,
    wgu,
    wd,
    gather,
    scatter,
    p_own,
    p_send,
    p_recv,
    y_send,
    y_recv,
    line_send,
    line_recv,
    opp_recv,
    far_send,
    far_recv,
    own_sum,
    send_sems,
    recv_sems,
    local_sems,
):
    q = d // QUARTERS
    section = lax.axis_index("section")
    ep = lax.axis_index("ep")
    z, low = ep // 4, ep % 4
    y, core = low // 2, low % 2
    g, i = z // LINE, z % LINE

    def at(to_z):
        return (section, to_z * 4 + low)

    plus4, minus4 = at((z + LINE) % NZ), at((z + NZ - LINE) % NZ)
    opp_first = LINE * ((g + 2) % EXPERTS)
    opp_rep = at(opp_first + jnp.where(i < 2, LINE - 1, 0))
    is_end = (i == 0) | (i == LINE - 1)
    served = jnp.where(i == 0, 2, 0)
    peers = [at(g * LINE + (i + m) % LINE) for m in range(1, LINE)]
    across = (section, ep + 2 - 4 * y)
    twin = (section, ep + 1 - 2 * core)
    up, down = (section + 1, ep), (section - 1, ep)
    not_last, not_first = section < ns - 1, section > 0

    load_gu = pltpu.make_async_copy(wgu_hbm.at[0], wgu_raw, local_sems.at[0])
    load_d = pltpu.make_async_copy(wd_hbm.at[0], wd, local_sems.at[1])

    barrier = pltpu.get_barrier_semaphore()

    def greet(device):
        pl.semaphore_signal(barrier, inc=1, device_id=device, device_id_type=MESH)

    greet(opp_rep)

    @pl.when(is_end)
    def _():
        greet(at(opp_first + served))
        greet(at(opp_first + served + 1))

    greet(plus4)
    greet(minus4)
    pl.when(not_last)(lambda: greet(up))
    pl.when(not_first)(lambda: greet(down))
    for peer in peers:
        greet(peer)
    greet(across)
    greet(twin)
    load_gu.start()
    load_d.start()

    used = [0]

    def sems(n=1):
        used[0] += n
        return used[0] - n

    def copy(src, dst, send_index, recv_index, device):
        return pltpu.make_async_remote_copy(
            src_ref=src,
            dst_ref=dst,
            send_sem=send_sems.at[send_index],
            recv_sem=recv_sems.at[recv_index],
            device_id=device,
            device_id_type=MESH,
        )

    def plain(src, dst, device):
        index = sems()
        return copy(src, dst, index, index, device)

    def arrived(dst, recv_index):
        copy(dst, dst, 0, recv_index, twin).wait_recv()

    for stream, tok in enumerate((tok_a, tok_b)):
        rows = tok[...].astype(F32)
        outgoing[stream] = jnp.concatenate(
            [rows[:, n * q : (n + 1) * q] for n in range(QUARTERS)], axis=0
        ).astype(BF16)

    relay_up = plain(outgoing.at[0], current.at[0], up)
    relay_down = plain(outgoing.at[1], current.at[1], down)

    pl.semaphore_wait(
        barrier,
        8
        + not_last.astype(jnp.int32)
        + not_first.astype(jnp.int32)
        + 2 * is_end.astype(jnp.int32),
    )
    pl.when(not_last)(relay_up.start)
    pl.when(not_first)(relay_down.start)

    @pl.when(section == 0)
    def _():
        current[0] = outgoing[0]

    @pl.when(section == ns - 1)
    def _():
        current[1] = outgoing[1]

    row, col = iota((64, 32), 0), iota((64, 32), 1)
    token, _ = find_tokens(
        (routes_a, routes_b), None, (row // 2) % 2, (g + row // 16) % EXPERTS, row % CAP
    )
    place = ((row // 2) % 2) * 16 + ((row // 4) % 4) * 4 + token
    picker = jnp.where(col == place, 1.0, 0.0).astype(BF16)

    lane = iota((1, 128), 1)
    token, gain = find_tokens(
        (routes_a, routes_b),
        (gains_a, gains_b),
        (lane // 2) % 2,
        (g + (lane // 16) % 4) % EXPERTS,
        lane % CAP,
    )
    high = gain.astype(BF16).astype(F32)
    weight = jnp.where(lane < 64, high, gain - high)
    row = iota((32, 128), 0)
    mine = (row % 4 == token) & ((row // 4) % 4 == (lane // 4) % 4) & (row // 16 == (lane // 2) % 2)
    mixing = jnp.where(mine, weight, 0.0).astype(BF16)

    row, col = iota((256, 256), 0), iota((256, 256), 1)
    place = ((row // 16) % 4) * 64 + ((row // 4) % 4) * 16 + (row // 64) * 4 + row % 4
    gather[...] = jnp.where(col == place, 1.0, 0.0).astype(BF16)
    row, col = iota((64, 64), 0), iota((64, 64), 1)
    place = ((row // 4) % 4) * 16 + (row // 16) * 4 + row % 4
    scatter[...] = jnp.where(col == place, 1.0, 0.0).astype(BF16)

    load_gu.wait()

    def unpack_weights(n, carry):
        rows = pl.ds(pl.multiple_of(n * 256, 256), 256)
        wgu[rows, :] = wgu_raw[rows].reshape(256, wgu.shape[1])
        return carry

    lax.fori_loop(0, d // 256, unpack_weights, 0)
    load_d.wait()

    pl.when(not_first)(relay_up.wait_recv)
    pl.when(not_last)(relay_down.wait_recv)

    picked = jnp.dot(picker, current[...].reshape(32, q), preferred_element_type=F32).astype(BF16)
    packed[0] = picked[32:48]
    far_sem, far_opp_recv = sems(), sems(2)
    far_opp = copy(
        packed.at[0], xin.at[0, 2 * LINE + i], far_sem, far_opp_recv + i % 2, opp_rep
    )
    far_opp.start()
    packed[1] = picked[16:32]
    packed[2] = picked[48:64]
    far_plus = plain(packed.at[1], xin.at[0, 3 * LINE + i], plus4)
    far_minus = plain(packed.at[2], xin.at[0, LINE + i], minus4)
    far_plus.start()
    far_minus.start()
    xin[0, i] = picked[0:16]

    started = [far_opp, far_plus, far_minus]

    line_sems = {}

    def line_out(o):
        line_sems[o] = sems(LINE - 1)
        for m in range(1, LINE):
            index = line_sems[o] + m - 1
            block = xin.at[0, o * LINE + i]
            out = copy(block, block, index, index, peers[m - 1])
            out.start()
            started.append(out)

    def line_in(o):
        for m in range(1, LINE):
            arrived(xin.at[0, o * LINE + (i + LINE - m) % LINE], line_sems[o] + m - 1)

    x_across, x_twin, x_far, p_twin, p_across = {}, {}, {}, {}, {}
    for o in range(EXPERTS):
        block = pl.ds(o * LINE, LINE)
        x_across[o] = plain(xin.at[0, block], xin.at[2, block], across)
        x_twin[o] = plain(xin.at[0, block], xin.at[1, block], twin)
        x_far[o] = plain(xin.at[2, block], xin.at[3, block], twin)
        p_twin[o] = plain(p_send.at[o], p_recv.at[o], twin)
        p_across[o] = plain(y_send.at[o], y_recv.at[o], across)
    for group in (x_across, x_twin, x_far, p_twin, p_across):
        started += list(group.values())

    def share(o):
        x_across[o].start()
        x_twin[o].start()

    def pass_on(o):
        x_across[o].wait_recv()
        x_far[o].start()

    def experts(o):
        x_twin[o].wait_recv()
        x_far[o].wait_recv()
        rows = xin[:, o * LINE : (o + 1) * LINE].reshape(256, q)
        sorted_rows = jnp.dot(gather[...], rows, preferred_element_type=F32).astype(BF16)
        projected = jnp.zeros((64, wgu.shape[1]), F32)
        for n in range(QUARTERS):
            projected += jnp.dot(
                sorted_rows[n * 64 : (n + 1) * 64],
                wgu[n * q : (n + 1) * q],
                preferred_element_type=F32,
            )
        gate, upper = projected[:, :128], projected[:, 128:]
        hidden = (gate * jax.nn.sigmoid(gate) * upper).astype(BF16)
        part = jnp.dot(hidden, wd[...], preferred_element_type=F32)
        p_send[o, 0] = part[16:32].astype(BF16)
        p_send[o, 1] = part[48:64].astype(BF16)
        p_twin[o].start()
        p_own[o, 0] = part[0:16]
        p_own[o, 1] = part[32:48]

    def sum_twins(o):
        p_twin[o].wait_recv()
        y_send[o] = (p_own[o, 1] + p_recv[o, 1].astype(F32)).astype(BF16)
        p_across[o].start()
        p_own[o, 0] = p_own[o, 0] + p_recv[o, 0].astype(F32)

    def to_blocks(o):
        p_across[o].wait_recv()
        total = (p_own[o, 0] + y_recv[o].astype(F32)).astype(BF16)
        stacked = jnp.concatenate([total[:, n * q : (n + 1) * q] for n in range(QUARTERS)], axis=0)
        blocks = jnp.dot(scatter[...], stacked, preferred_element_type=F32).astype(BF16)
        line_send[o] = blocks.reshape(LINE, 16, q)

    back_sems = {}

    def line_back(o):
        back_sems[o] = sems(LINE - 1)
        for m in range(1, LINE):
            index = back_sems[o] + m - 1
            out = copy(
                line_send.at[o, (i + m) % LINE], line_recv.at[o, m - 1], index, index, peers[m - 1]
            )
            out.start()
            started.append(out)

    def line_sum(o):
        total = line_send[o, i].astype(F32)
        for m in range(1, LINE):
            arrived(line_recv.at[o, m - 1], back_sems[o] + m - 1)
            total = total + line_recv[o, m - 1].astype(F32)
        return total.astype(BF16)

    line_out(0)
    line_in(0)
    share(0)
    far_minus.wait_recv()
    line_out(1)
    far_plus.wait_recv()
    line_out(3)

    opp_send, opp_from = sems(LINE - 1), sems(2)
    half_block = xin.at[0, pl.ds(2 * LINE + served, 2)]
    opp_line = [
        copy(half_block, half_block, opp_send + m, opp_from + jnp.where(i == 0, 0, 1), peers[m])
        for m in range(LINE - 1)
    ]

    @pl.when(is_end)
    def _():
        arrived(xin.at[0, 2 * LINE + served], far_opp_recv)
        arrived(xin.at[0, 2 * LINE + served + 1], far_opp_recv + 1)
        for out in opp_line:
            out.start()

    pass_on(0)
    experts(0)
    line_in(1)
    share(1)
    line_in(3)
    share(3)

    @pl.when(i != 0)
    def _():
        arrived(xin.at[0, pl.ds(2 * LINE + 2, 2)], opp_from)

    @pl.when(i != LINE - 1)
    def _():
        arrived(xin.at[0, pl.ds(2 * LINE, 2)], opp_from + 1)

    share(2)
    sum_twins(0)
    pass_on(1)
    experts(1)
    pass_on(3)
    experts(3)
    to_blocks(0)
    line_back(0)
    sum_twins(1)
    sum_twins(3)
    pass_on(2)
    experts(2)
    sum_twins(2)
    to_blocks(1)
    line_back(1)
    to_blocks(3)
    line_back(3)
    to_blocks(2)

    opp_back, opp_back_recv = sems(2), sems(LINE - 1)
    away0, away3 = (LINE - i) % LINE, LINE - 1 - i
    to_first = copy(
        line_send.at[2, pl.ds(2, 2)],
        opp_recv.at[jnp.maximum(away0 - 1, 0)],
        opp_back,
        opp_back_recv + jnp.maximum(away0 - 1, 0),
        at(g * LINE),
    )
    to_final = copy(
        line_send.at[2, pl.ds(0, 2)],
        opp_recv.at[jnp.maximum(away3 - 1, 0)],
        opp_back + 1,
        opp_back_recv + jnp.maximum(away3 - 1, 0),
        at(g * LINE + LINE - 1),
    )
    pl.when(i != 0)(to_first.start)
    pl.when(i != LINE - 1)(to_final.start)

    far_send[0] = line_sum(1)
    return_plus = plain(far_send.at[0], far_recv.at[2], plus4)
    return_plus.start()
    far_send[1] = line_sum(3)
    return_minus = plain(far_send.at[1], far_recv.at[0], minus4)
    return_minus.start()
    started += [return_plus, return_minus]

    return_opp, return_opp_recv = sems(2), sems()
    returns = [
        copy(
            far_send.at[2 + n],
            far_recv.at[1],
            return_opp + n,
            return_opp_recv,
            at(opp_first + served + n),
        )
        for n in range(2)
    ]

    @pl.when(is_end)
    def _():
        total = line_send[2, pl.ds(served, 2)].astype(F32)
        for m in range(LINE - 1):
            arrived(opp_recv.at[m], opp_back_recv + m)
            total = total + opp_recv[m].astype(F32)
        far_send[2:4] = total.astype(BF16)
        for out in returns:
            out.start()

    own_sum[...] = line_sum(0)

    pl.when(not_last)(relay_up.wait_send)
    pl.when(not_first)(relay_down.wait_send)
    for out in started:
        out.wait_send()

    @pl.when(is_end)
    def _():
        for out in opp_line + returns:
            out.wait_send()

    pl.when(i != 0)(to_first.wait_send)
    pl.when(i != LINE - 1)(to_final.wait_send)

    return_plus.wait_recv()
    return_minus.wait_recv()
    arrived(far_recv.at[1], return_opp_recv)
    parts = jnp.concatenate([own_sum[...]] + [far_recv[n] for n in range(3)], axis=0)
    added = jnp.dot(mixing, jnp.concatenate([parts, parts], axis=0), preferred_element_type=F32)
    mixed = current[...].reshape(32, q).astype(F32) + added
    for s, out in enumerate((out_a, out_b)):
        for n in range(QUARTERS):
            first = s * 16 + n * TOK
            out[:, n * q : (n + 1) * q] = mixed[first : first + TOK].astype(BF16)


def shards(ns, *args):
    tokens_a = args[0]
    d = tokens_a.shape[1]
    q = d // QUARTERS
    width = args[7].shape[1]
    vmem = pl.BlockSpec(memory_space=pltpu.VMEM)
    smem = pl.BlockSpec(memory_space=pltpu.SMEM)
    hbm = pl.BlockSpec(memory_space=pl.ANY)
    small = [array.T for array in args[2:6]]
    return pl.pallas_call(
        functools.partial(kernel, ns, d),
        out_shape=[jax.ShapeDtypeStruct(tokens_a.shape, BF16)] * 2,
        in_specs=[vmem] * 2 + [smem] * 4 + [hbm] * 2,
        out_specs=[vmem] * 2,
        scratch_shapes=[
            pltpu.VMEM((2, 16, q), BF16),
            pltpu.VMEM((2, 16, q), BF16),
            pltpu.VMEM((3, 16, q), BF16),
            pltpu.VMEM((4, NZ, 16, q), BF16),
            pltpu.VMEM((d, 2, width), BF16),
            pltpu.VMEM((d, 2 * width), BF16),
            pltpu.VMEM((width, d), BF16),
            pltpu.VMEM((256, 256), BF16),
            pltpu.VMEM((64, 64), BF16),
            pltpu.VMEM((EXPERTS, 2, 16, d), F32),
            pltpu.VMEM((EXPERTS, 2, 16, d), BF16),
            pltpu.VMEM((EXPERTS, 2, 16, d), BF16),
            pltpu.VMEM((EXPERTS, 16, d), BF16),
            pltpu.VMEM((EXPERTS, 16, d), BF16),
            pltpu.VMEM((EXPERTS, LINE, 16, q), BF16),
            pltpu.VMEM((EXPERTS, LINE - 1, 16, q), BF16),
            pltpu.VMEM((LINE - 1, 2, 16, q), BF16),
            pltpu.VMEM((4, 16, q), BF16),
            pltpu.VMEM((3, 16, q), BF16),
            pltpu.VMEM((16, q), BF16),
            pltpu.SemaphoreType.DMA((N_SEMS,)),
            pltpu.SemaphoreType.DMA((N_SEMS,)),
            pltpu.SemaphoreType.DMA((2,)),
        ],
        compiler_params=pltpu.CompilerParams(
            collective_id=0, has_side_effects=True, vmem_limit_bytes=60 * 1024 * 1024
        ),
    )(*args[:2], *small, *args[6:])


def solution(mesh):
    ns = mesh.shape["section"]
    rows = P(("section", "ep"), None)
    in_specs = (rows,) * 6 + (P("section", None, None, "ep"), P("section", "ep", None))
    return jax.shard_map(
        functools.partial(shards, ns),
        mesh=mesh,
        in_specs=in_specs,
        out_specs=(rows, rows),
        check_vma=False,
    )
```

time: 253 us -> 78.8 us (0.31)
  the two profiles are of different devices: /device:TPU:1 before, /device:TPU:6 now
where the time goes in v2:
time: 78.8 us; the launch traced here: 78.4 us
  Pallas kernels  75.1 us (95%)
  local copies, waits for them, and re-layouts  2.74 us (3%)
    pallas_call x1, Pallas kernels, shards(): pl.pallas_call(functools.partial(kernel, ns, d), out_shape=[jax.ShapeDtyp...  75.1 us
    unnamed x2, local copies, waits for them, and re-layouts  2.74 us

profile of v2, /device:TPU:6, one launch (start us, length us, event | category | flops | bytes accessed | tf_op | source)
XLA Modules:
  0.0 78.4 jit_solution(12570416311457835932)
XLA Ops:
  0.6 75.1 %shard_map.95 = (bf16[4,3584]{1,0:T(4,128)(2,1)}, bf16[4,3584]{1,0:T(4,128)(2,1)}) custom-call(bf16[4,3584]{1,0:T(4,128)(2,1)} %tok_a.1, bf16[4,3584]{1,0:T(4,128)(2,1)} %tok_b.1, s32[2,4]{1,0:T(2,128)} %bitcast.4, s32[2,4]{1,0:T(2,128)} %bitcast.5, f32[2,4]{1,0:T(2,128)} %bitcast.6, f32[2,4]{1,0:T(2,128)} %bitcast.7, bf16[1,3584,2,128]{3,2,1,0:T(2,128)(2,1)} %wgu_hbm.1, ...), custom_call_target="tpu_custom_call" | custom-call | tf_op jit(solution)/shard_map/pallas_call | solution.py:464
  75.7 1.4 %copy.12 = bf16[4,3584]{1,0:T(4,128)(2,1)} copy(bf16[4,3584]{1,0:T(4,128)(2,1)} %get-tuple-element.4) | data formatting | bytes 57344
  77.1 1.4 %copy.13 = bf16[4,3584]{1,0:T(4,128)(2,1)} copy(bf16[4,3584]{1,0:T(4,128)(2,1)} %get-tuple-element.5) | data formatting | bytes 57344

commit v3 on v2

--- a/solution.py
+++ b/solution.py
@@ -70,13 +70,13 @@
     y_recv,
     line_send,
     line_recv,
-    opp_recv,
     far_send,
     far_recv,
     own_sum,
     send_sems,
     recv_sems,
     local_sems,
+    met,
 ):
     q = d // QUARTERS
     section = lax.axis_index("section")
@@ -89,10 +89,8 @@
         return (section, to_z * 4 + low)
 
     plus4, minus4 = at((z + LINE) % NZ), at((z + NZ - LINE) % NZ)
-    opp_first = LINE * ((g + 2) % EXPERTS)
-    opp_rep = at(opp_first + jnp.where(i < 2, LINE - 1, 0))
-    is_end = (i == 0) | (i == LINE - 1)
-    served = jnp.where(i == 0, 2, 0)
+    opposite_z = LINE * ((g + 2) % EXPERTS) + LINE - 1 - i
+    opposite = at(opposite_z)
     peers = [at(g * LINE + (i + m) % LINE) for m in range(1, LINE)]
     across = (section, ep + 2 - 4 * y)
     twin = (section, ep + 1 - 2 * core)
@@ -104,24 +102,21 @@
 
     barrier = pltpu.get_barrier_semaphore()
 
-    def greet(device):
-        pl.semaphore_signal(barrier, inc=1, device_id=device, device_id_type=MESH)
-
-    greet(opp_rep)
-
-    @pl.when(is_end)
-    def _():
-        greet(at(opp_first + served))
-        greet(at(opp_first + served + 1))
-
-    greet(plus4)
-    greet(minus4)
-    pl.when(not_last)(lambda: greet(up))
-    pl.when(not_first)(lambda: greet(down))
-    for peer in peers:
-        greet(peer)
-    greet(across)
-    greet(twin)
+    def signal(semaphore, device):
+        pl.semaphore_signal(semaphore, inc=1, device_id=device, device_id_type=MESH)
+
+    def greet(to_section, to_z, to_y, to_core):
+        signal(barrier, (to_section, to_z * 4 + to_y * 2 + to_core))
+
+    greet(section, opposite_z, y, 1)
+    greet(section, (z + LINE) % NZ, y, 1)
+    greet(section, (z + NZ - LINE) % NZ, y, 1)
+    pl.when(not_last)(lambda: greet(section + 1, z, y, 0))
+    pl.when(not_first)(lambda: greet(section - 1, z, y, 0))
+    for m in range(1, LINE):
+        greet(section, g * LINE + (i + m) % LINE, y, 0)
+    greet(section, z, 1 - y, 0)
+    signal(barrier, twin)
     load_gu.start()
     load_d.start()
 
@@ -157,13 +152,18 @@
     relay_up = plain(outgoing.at[0], current.at[0], up)
     relay_down = plain(outgoing.at[1], current.at[1], down)
 
-    pl.semaphore_wait(
-        barrier,
-        8
-        + not_last.astype(jnp.int32)
-        + not_first.astype(jnp.int32)
-        + 2 * is_end.astype(jnp.int32),
-    )
+    near = 2 * (LINE + not_last.astype(jnp.int32) + not_first.astype(jnp.int32)) + 1
+    far = 2 * 3 + 1
+
+    @pl.when(core == 0)
+    def _():
+        pl.semaphore_wait(barrier, near)
+        signal(met, twin)
+
+    @pl.when(core == 1)
+    def _():
+        pl.semaphore_wait(met, 1)
+
     pl.when(not_last)(relay_up.start)
     pl.when(not_first)(relay_down.start)
 
@@ -217,54 +217,50 @@
     pl.when(not_last)(relay_down.wait_recv)
 
     picked = jnp.dot(picker, current[...].reshape(32, q), preferred_element_type=F32).astype(BF16)
+    xin[0, i] = picked[0:16]
     packed[0] = picked[32:48]
-    far_sem, far_opp_recv = sems(), sems(2)
-    far_opp = copy(
-        packed.at[0], xin.at[0, 2 * LINE + i], far_sem, far_opp_recv + i % 2, opp_rep
-    )
-    far_opp.start()
     packed[1] = picked[16:32]
     packed[2] = picked[48:64]
+    far_opp = plain(packed.at[0], xin.at[0, 2 * LINE + i], opposite)
     far_plus = plain(packed.at[1], xin.at[0, 3 * LINE + i], plus4)
     far_minus = plain(packed.at[2], xin.at[0, LINE + i], minus4)
-    far_plus.start()
-    far_minus.start()
-    xin[0, i] = picked[0:16]
-
     started = [far_opp, far_plus, far_minus]
 
-    line_sems = {}
+    def held(o, j):
+        return 2 * LINE + LINE - 1 - j if o == 2 else o * LINE + j
+
+    x_across, x_twin, x_far, p_twin, p_across, line_sems = {}, {}, {}, {}, {}, {}
+    for o in range(EXPERTS):
+        block = pl.ds(o * LINE, LINE)
+        x_across[o] = []
+        for m in range(LINE):
+            place = held(o, (i + LINE - m) % LINE)
+            x_across[o].append(plain(xin.at[0, place], xin.at[2, place], across))
+        x_twin[o] = plain(xin.at[0, block], xin.at[1, block], twin)
+        x_far[o] = plain(xin.at[2, block], xin.at[3, block], twin)
+        p_twin[o] = plain(p_send.at[o], p_recv.at[o], twin)
+        p_across[o] = plain(y_send.at[o], y_recv.at[o], across)
+        started += x_across[o] + [x_twin[o], x_far[o], p_twin[o], p_across[o]]
 
     def line_out(o):
         line_sems[o] = sems(LINE - 1)
         for m in range(1, LINE):
             index = line_sems[o] + m - 1
-            block = xin.at[0, o * LINE + i]
+            block = xin.at[0, held(o, i)]
             out = copy(block, block, index, index, peers[m - 1])
             out.start()
             started.append(out)
+        x_across[o][0].start()
 
     def line_in(o):
         for m in range(1, LINE):
-            arrived(xin.at[0, o * LINE + (i + LINE - m) % LINE], line_sems[o] + m - 1)
-
-    x_across, x_twin, x_far, p_twin, p_across = {}, {}, {}, {}, {}
-    for o in range(EXPERTS):
-        block = pl.ds(o * LINE, LINE)
-        x_across[o] = plain(xin.at[0, block], xin.at[2, block], across)
-        x_twin[o] = plain(xin.at[0, block], xin.at[1, block], twin)
-        x_far[o] = plain(xin.at[2, block], xin.at[3, block], twin)
-        p_twin[o] = plain(p_send.at[o], p_recv.at[o], twin)
-        p_across[o] = plain(y_send.at[o], y_recv.at[o], across)
-    for group in (x_across, x_twin, x_far, p_twin, p_across):
-        started += list(group.values())
-
-    def share(o):
-        x_across[o].start()
+            arrived(xin.at[0, held(o, (i + LINE - m) % LINE)], line_sems[o] + m - 1)
+            x_across[o][m].start()
         x_twin[o].start()
 
     def pass_on(o):
-        x_across[o].wait_recv()
+        for part in x_across[o]:
+            part.wait_recv()
         x_far[o].start()
 
     def experts(o):
@@ -307,57 +303,44 @@
         back_sems[o] = sems(LINE - 1)
         for m in range(1, LINE):
             index = back_sems[o] + m - 1
-            out = copy(
-                line_send.at[o, (i + m) % LINE], line_recv.at[o, m - 1], index, index, peers[m - 1]
-            )
+            block = held(o, (i + m) % LINE) - o * LINE
+            out = copy(line_send.at[o, block], line_recv.at[o, m - 1], index, index, peers[m - 1])
             out.start()
             started.append(out)
 
     def line_sum(o):
-        total = line_send[o, i].astype(F32)
+        total = line_send[o, held(o, i) - o * LINE].astype(F32)
         for m in range(1, LINE):
             arrived(line_recv.at[o, m - 1], back_sems[o] + m - 1)
             total = total + line_recv[o, m - 1].astype(F32)
         return total.astype(BF16)
 
     line_out(0)
+
+    @pl.when(core == 1)
+    def _():
+        pl.semaphore_wait(barrier, far)
+        signal(met, twin)
+
+    @pl.when(core == 0)
+    def _():
+        pl.semaphore_wait(met, 1)
+
+    far_opp.start()
+    far_plus.start()
+    far_minus.start()
     line_in(0)
-    share(0)
     far_minus.wait_recv()
     line_out(1)
     far_plus.wait_recv()
     line_out(3)
-
-    opp_send, opp_from = sems(LINE - 1), sems(2)
-    half_block = xin.at[0, pl.ds(2 * LINE + served, 2)]
-    opp_line = [
-        copy(half_block, half_block, opp_send + m, opp_from + jnp.where(i == 0, 0, 1), peers[m])
-        for m in range(LINE - 1)
-    ]
-
-    @pl.when(is_end)
-    def _():
-        arrived(xin.at[0, 2 * LINE + served], far_opp_recv)
-        arrived(xin.at[0, 2 * LINE + served + 1], far_opp_recv + 1)
-        for out in opp_line:
-            out.start()
-
+    far_opp.wait_recv()
+    line_out(2)
     pass_on(0)
     experts(0)
     line_in(1)
-    share(1)
     line_in(3)
-    share(3)
-
-    @pl.when(i != 0)
-    def _():
-        arrived(xin.at[0, pl.ds(2 * LINE + 2, 2)], opp_from)
-
-    @pl.when(i != LINE - 1)
-    def _():
-        arrived(xin.at[0, pl.ds(2 * LINE, 2)], opp_from + 1)
-
-    share(2)
+    line_in(2)
     sum_twins(0)
     pass_on(1)
     experts(1)
@@ -375,55 +358,14 @@
     to_blocks(3)
     line_back(3)
     to_blocks(2)
-
-    opp_back, opp_back_recv = sems(2), sems(LINE - 1)
-    away0, away3 = (LINE - i) % LINE, LINE - 1 - i
-    to_first = copy(
-        line_send.at[2, pl.ds(2, 2)],
-        opp_recv.at[jnp.maximum(away0 - 1, 0)],
-        opp_back,
-        opp_back_recv + jnp.maximum(away0 - 1, 0),
-        at(g * LINE),
-    )
-    to_final = copy(
-        line_send.at[2, pl.ds(0, 2)],
-        opp_recv.at[jnp.maximum(away3 - 1, 0)],
-        opp_back + 1,
-        opp_back_recv + jnp.maximum(away3 - 1, 0),
-        at(g * LINE + LINE - 1),
-    )
-    pl.when(i != 0)(to_first.start)
-    pl.when(i != LINE - 1)(to_final.start)
-
-    far_send[0] = line_sum(1)
-    return_plus = plain(far_send.at[0], far_recv.at[2], plus4)
-    return_plus.start()
-    far_send[1] = line_sum(3)
-    return_minus = plain(far_send.at[1], far_recv.at[0], minus4)
-    return_minus.start()
-    started += [return_plus, return_minus]
-
-    return_opp, return_opp_recv = sems(2), sems()
-    returns = [
-        copy(
-            far_send.at[2 + n],
-            far_recv.at[1],
-            return_opp + n,
-            return_opp_recv,
-            at(opp_first + served + n),
-        )
-        for n in range(2)
-    ]
-
-    @pl.when(is_end)
-    def _():
-        total = line_send[2, pl.ds(served, 2)].astype(F32)
-        for m in range(LINE - 1):
-            arrived(opp_recv.at[m], opp_back_recv + m)
-            total = total + opp_recv[m].astype(F32)
-        far_send[2:4] = total.astype(BF16)
-        for out in returns:
-            out.start()
+    line_back(2)
+
+    returns = []
+    for o, slot, device in ((1, 2, plus4), (3, 0, minus4), (2, 1, opposite)):
+        far_send[o - 1] = line_sum(o)
+        returns.append(plain(far_send.at[o - 1], far_recv.at[slot], device))
+        returns[-1].start()
+    started += returns
 
     own_sum[...] = line_sum(0)
 
@@ -432,17 +374,8 @@
     for out in started:
         out.wait_send()
 
-    @pl.when(is_end)
-    def _():
-        for out in opp_line + returns:
-            out.wait_send()
-
-    pl.when(i != 0)(to_first.wait_send)
-    pl.when(i != LINE - 1)(to_final.wait_send)
-
-    return_plus.wait_recv()
-    return_minus.wait_recv()
-    arrived(far_recv.at[1], return_opp_recv)
+    for out in returns:
+        out.wait_recv()
     parts = jnp.concatenate([own_sum[...]] + [far_recv[n] for n in range(3)], axis=0)
     added = jnp.dot(mixing, jnp.concatenate([parts, parts], axis=0), preferred_element_type=F32)
     mixed = current[...].reshape(32, q).astype(F32) + added
@@ -483,13 +416,13 @@
             pltpu.VMEM((EXPERTS, 16, d), BF16),
             pltpu.VMEM((EXPERTS, LINE, 16, q), BF16),
             pltpu.VMEM((EXPERTS, LINE - 1, 16, q), BF16),
-            pltpu.VMEM((LINE - 1, 2, 16, q), BF16),
-            pltpu.VMEM((4, 16, q), BF16),
+            pltpu.VMEM((3, 16, q), BF16),
             pltpu.VMEM((3, 16, q), BF16),
             pltpu.VMEM((16, q), BF16),
             pltpu.SemaphoreType.DMA((N_SEMS,)),
             pltpu.SemaphoreType.DMA((N_SEMS,)),
             pltpu.SemaphoreType.DMA((2,)),
+            pltpu.SemaphoreType.REGULAR,
         ],
         compiler_params=pltpu.CompilerParams(
             collective_id=0, has_side_effects=True, vmem_limit_bytes=60 * 1024 * 1024

time: 78.8 us -> 76.2 us (0.967)
  the two profiles are of different devices: /device:TPU:6 before, /device:TPU:1 now
where the time goes in v3:
time: 76.2 us; the launch traced here: 75.8 us
  Pallas kernels  72.4 us (95%)
  local copies, waits for them, and re-layouts  2.74 us (4%)
    pallas_call x1, Pallas kernels, shards(): pl.pallas_call(functools.partial(kernel, ns, d), out_shape=[jax.ShapeDtyp...  72.4 us
    unnamed x2, local copies, waits for them, and re-layouts  2.74 us

profile of v3, /device:TPU:1, one launch (start us, length us, event | category | flops | bytes accessed | tf_op | source)
XLA Modules:
  0.0 75.8 jit_solution(16181903828257876001)
XLA Ops:
  0.6 72.4 %shard_map.95 = (bf16[4,3584]{1,0:T(4,128)(2,1)}, bf16[4,3584]{1,0:T(4,128)(2,1)}) custom-call(bf16[4,3584]{1,0:T(4,128)(2,1)} %tok_a.1, bf16[4,3584]{1,0:T(4,128)(2,1)} %tok_b.1, s32[2,4]{1,0:T(2,128)} %bitcast.4, s32[2,4]{1,0:T(2,128)} %bitcast.5, f32[2,4]{1,0:T(2,128)} %bitcast.6, f32[2,4]{1,0:T(2,128)} %bitcast.7, bf16[1,3584,2,128]{3,2,1,0:T(2,128)(2,1)} %wgu_hbm.1, ...), custom_call_target="tpu_custom_call" | custom-call | tf_op jit(solution)/shard_map/pallas_call | solution.py:397
  73.1 1.4 %copy.12 = bf16[4,3584]{1,0:T(4,128)(2,1)} copy(bf16[4,3584]{1,0:T(4,128)(2,1)} %get-tuple-element.4) | data formatting | bytes 57344
  74.5 1.4 %copy.13 = bf16[4,3584]{1,0:T(4,128)(2,1)} copy(bf16[4,3584]{1,0:T(4,128)(2,1)} %get-tuple-element.5) | data formatting | bytes 57344

commit v4 on v3

--- a/solution.py
+++ b/solution.py
@@ -52,8 +52,7 @@
     gains_b,
     wgu_hbm,
     wd_hbm,
-    out_a,
-    out_b,
+    result,
     outgoing,
     current,
     packed,
@@ -379,10 +378,10 @@
     parts = jnp.concatenate([own_sum[...]] + [far_recv[n] for n in range(3)], axis=0)
     added = jnp.dot(mixing, jnp.concatenate([parts, parts], axis=0), preferred_element_type=F32)
     mixed = current[...].reshape(32, q).astype(F32) + added
-    for s, out in enumerate((out_a, out_b)):
+    for s in range(2):
         for n in range(QUARTERS):
             first = s * 16 + n * TOK
-            out[:, n * q : (n + 1) * q] = mixed[first : first + TOK].astype(BF16)
+            result[s, :, n * q : (n + 1) * q] = mixed[first : first + TOK].astype(BF16)
 
 
 def shards(ns, *args):
@@ -394,11 +393,11 @@
     smem = pl.BlockSpec(memory_space=pltpu.SMEM)
     hbm = pl.BlockSpec(memory_space=pl.ANY)
     small = [array.T for array in args[2:6]]
-    return pl.pallas_call(
+    mixed = pl.pallas_call(
         functools.partial(kernel, ns, d),
-        out_shape=[jax.ShapeDtypeStruct(tokens_a.shape, BF16)] * 2,
+        out_shape=jax.ShapeDtypeStruct((2,) + tokens_a.shape, BF16),
         in_specs=[vmem] * 2 + [smem] * 4 + [hbm] * 2,
-        out_specs=[vmem] * 2,
+        out_specs=vmem,
         scratch_shapes=[
             pltpu.VMEM((2, 16, q), BF16),
             pltpu.VMEM((2, 16, q), BF16),
@@ -428,6 +427,7 @@
             collective_id=0, has_side_effects=True, vmem_limit_bytes=60 * 1024 * 1024
         ),
     )(*args[:2], *small, *args[6:])
+    return mixed[0], mixed[1]
 
 
 def solution(mesh):

time: 76.2 us -> 74.8 us (0.982)
  local copies, waits for them, and re-layouts: 2.74 us -> 1.41 us
    unnamed x2 -> x0, local copies, waits for them, and re-layouts: 2.74 us -> none
    squeeze x0 -> x1, local copies, waits for them, and re-layouts: none -> 1.41 us  [shards(): return (mixed[0], mixed[1])]
where the time goes in v4:
time: 74.8 us; the launch traced here: 74.5 us
  Pallas kernels  72.4 us (97%)
  local copies, waits for them, and re-layouts  1.41 us (2%)
    pallas_call x1, Pallas kernels, shards(): pl.pallas_call(functools.partial(kernel, ns, d), out_shape=jax.ShapeDtype...  72.4 us

profile of v4, /device:TPU:1, one launch (start us, length us, event | category | flops | bytes accessed | tf_op | source)
XLA Modules:
  0.0 74.5 jit_solution(7530969259310338836)
XLA Ops:
  0.6 72.4 %shard_map.95 = bf16[2,4,3584]{2,1,0:T(4,128)(2,1)} custom-call(bf16[4,3584]{1,0:T(4,128)(2,1)} %tok_a.1, bf16[4,3584]{1,0:T(4,128)(2,1)} %tok_b.1, s32[2,4]{1,0:T(2,128)} %bitcast.8, s32[2,4]{1,0:T(2,128)} %bitcast.9, f32[2,4]{1,0:T(2,128)} %bitcast.10, f32[2,4]{1,0:T(2,128)} %bitcast.11, bf16[1,3584,2,128]{3,2,1,0:T(2,128)(2,1)} %wgu_hbm.1, ...), custom_call_target="tpu_custom_call" | custom-call | tf_op jit(solution)/shard_map/pallas_call | solution.py:396
  73.1 1.4 %slice_bitcast_fusion = (bf16[4,3584]{1,0:T(4,128)(2,1)}, bf16[4,3584]{1,0:T(4,128)(2,1)}) fusion(bf16[2,4,3584]{2,1,0:T(4,128)(2,1)} %shard_map.95), kind=kLoop, calls=%fused_computation | loop fusion | bytes 114688 | tf_op jit(solution)/shard_map/squeeze | solution.py:430

commit v5 on v4

--- a/solution.py
+++ b/solution.py
@@ -373,11 +373,23 @@
     for out in started:
         out.wait_send()
 
-    for out in returns:
-        out.wait_recv()
-    parts = jnp.concatenate([own_sum[...]] + [far_recv[n] for n in range(3)], axis=0)
-    added = jnp.dot(mixing, jnp.concatenate([parts, parts], axis=0), preferred_element_type=F32)
-    mixed = current[...].reshape(32, q).astype(F32) + added
+    def mix(weights, part):
+        twice = jnp.concatenate([part, part], axis=0)
+        return jnp.dot(weights, twice, preferred_element_type=F32)
+
+    def weights_of(first, last):
+        return jnp.concatenate([mixing[:, first:last], mixing[:, 64 + first : 64 + last]], axis=1)
+
+    late = weights_of(32, 48)
+    returns[0].wait_recv()
+    returns[1].wait_recv()
+    parts = jnp.concatenate([own_sum[...], far_recv[0], far_recv[2]], axis=0)
+    early = jnp.concatenate([weights_of(0, 32), weights_of(48, 64)], axis=1)
+    parts = jnp.concatenate([parts[0:32], parts[0:32], parts[32:48], parts[32:48]], axis=0)
+    mixed = current[...].reshape(32, q).astype(F32)
+    mixed = mixed + jnp.dot(early, parts, preferred_element_type=F32)
+    returns[2].wait_recv()
+    mixed = mixed + mix(late, far_recv[1])
     for s in range(2):
         for n in range(QUARTERS):
             first = s * 16 + n * TOK

time: 74.8 us -> 74.8 us (level)
  no operation moved by 1% of the time
where the time goes in v5:
time: 74.8 us; the launch traced here: 74.5 us
  Pallas kernels  72.5 us (97%)
  local copies, waits for them, and re-layouts  1.41 us (2%)
    pallas_call x1, Pallas kernels, shards(): pl.pallas_call(functools.partial(kernel, ns, d), out_shape=jax.ShapeDtype...  72.5 us

profile of v5, /device:TPU:1, one launch (start us, length us, event | category | flops | bytes accessed | tf_op | source)
XLA Modules:
  0.0 74.5 jit_solution(17609515241966522982)
XLA Ops:
  0.6 72.5 %shard_map.95 = bf16[2,4,3584]{2,1,0:T(4,128)(2,1)} custom-call(bf16[4,3584]{1,0:T(4,128)(2,1)} %tok_a.1, bf16[4,3584]{1,0:T(4,128)(2,1)} %tok_b.1, s32[2,4]{1,0:T(2,128)} %bitcast.8, s32[2,4]{1,0:T(2,128)} %bitcast.9, f32[2,4]{1,0:T(2,128)} %bitcast.10, f32[2,4]{1,0:T(2,128)} %bitcast.11, bf16[1,3584,2,128]{3,2,1,0:T(2,128)(2,1)} %wgu_hbm.1, ...), custom_call_target="tpu_custom_call" | custom-call | tf_op jit(solution)/shard_map/pallas_call | solution.py:408
  73.1 1.4 %slice_bitcast_fusion = (bf16[4,3584]{1,0:T(4,128)(2,1)}, bf16[4,3584]{1,0:T(4,128)(2,1)}) fusion(bf16[2,4,3584]{2,1,0:T(4,128)(2,1)} %shard_map.95), kind=kLoop, calls=%fused_computation | loop fusion | bytes 114688 | tf_op jit(solution)/shard_map/squeeze | solution.py:442
